TPU v7x, 32 devices: a whole 2x2x4 slice. The times are simulated.
32 devices in a mesh: table: 16 (over z, y, x), score: 2 (over core).
Axes of the slice: x: 2, y: 2, z: 4, core: 2. Of those that a mesh axis runs over, the one named last changes fastest.
Arguments:
- hot_item_table: float32 [2048, 128], replicated, may hold values from -6 to 6
- cold_item_table: float32 [16384, 128], P('table'), may hold values from -6 to 6
- hist_rows: int32 [128, 512], P('table', 'score'), may hold values from 0 to 18431, as said below
- cand_rows: int32 [128, 512], P('table', 'score'), may hold values from 0 to 18431, as said below
- w_query: bfloat16 [128, 128], replicated, may hold values from -0.5 to 0.5
- w_key: bfloat16 [128, 128], replicated, may hold values from -0.5 to 0.5
- w_first: bfloat16 [256, 1024], replicated, may hold values from -0.5 to 0.5
- w_second: bfloat16 [1, 1024, 1024], replicated, may hold values from -0.25 to 0.25
- w_out: bfloat16 [1024], replicated, may hold values from -0.25 to 0.25
Outputs:
- scores: float32 [128, 512], P('table', 'score')
Inputs may be any that keep to these rules, and one draw needn't show every extreme that they name: `hist_rows`: among the history items of one device (8 requests, 256 items each), at most 128 name cold rows of any one owner; for each index along score, one owner is named exactly 128 times by every device along table. `cand_rows`: among the candidates of one device (8 requests, 256 candidates each), at most 128 name cold rows of any one owner; for each index along score, one owner is named exactly 128 times by every device along table.
All inputs are finite; a program needn't handle non-finite values.
Results may differ from a plain program's by a relative error of at most 0.0072.
Values may be sent and summed in bfloat16 or wider, within the bound.
A program may use at most 64 MiB of HBM per device.

v0:
```python
import math
import jax
import jax.numpy as jnp
from jax import lax
from jax.sharding import PartitionSpec as P

H = 512
HOT = 2048
COLD_DEV = 1024


def owner_positions(owner_match):
    item_total, owner_count = owner_match.shape
    block = math.gcd(item_total, 128)
    blocks = item_total // block
    match_bf = owner_match.astype(jnp.bfloat16).reshape(blocks, block, owner_count)
    lower = (
        lax.broadcasted_iota(jnp.int32, (block, block), 0)
        > lax.broadcasted_iota(jnp.int32, (block, block), 1)
    ).astype(jnp.bfloat16)
    within = jnp.einsum("ij,kjo->kio", lower, match_bf, preferred_element_type=jnp.float32)
    totals = jnp.sum(match_bf.astype(jnp.float32), axis=1)
    earlier = (
        lax.broadcasted_iota(jnp.int32, (blocks, blocks), 0)
        > lax.broadcasted_iota(jnp.int32, (blocks, blocks), 1)
    ).astype(jnp.float32)
    offsets = jnp.einsum(
        "bk,ko->bo",
        earlier,
        totals,
        precision=lax.Precision.HIGHEST,
        preferred_element_type=jnp.float32,
    )
    before = (within + offsets[:, None, :]).reshape(item_total, owner_count)
    return jnp.sum(before * owner_match, axis=1).astype(jnp.int32)


def gather_owner_rows(
    grouped_item_codes, owner_capacity_list, hot_item_table, cold_item_table, table_row_count
):
    owner_iota = jnp.arange(table_row_count, dtype=jnp.int32)
    layouts = []
    outgoing = []
    for item_row_codes, slot_capacity in zip(grouped_item_codes, owner_capacity_list):
        is_cold = item_row_codes >= HOT
        relative = jnp.where(is_cold, item_row_codes - HOT, 0)
        owner_id = relative // COLD_DEV
        slot_id = relative % COLD_DEV
        owner_match = jnp.logical_and(
            owner_id[:, None] == owner_iota[None, :], is_cold[:, None]
        ).astype(jnp.float32)
        position = owner_positions(owner_match)
        flat_index = owner_id * slot_capacity + position
        slot_onehot = (
            position[:, None] == jnp.arange(slot_capacity, dtype=jnp.int32)[None, :]
        ).astype(jnp.float32)
        weighted = owner_match * slot_id.astype(jnp.float32)[:, None]
        requests_out = jnp.einsum(
            "io,is->os",
            weighted,
            slot_onehot,
            precision=lax.Precision.HIGHEST,
            preferred_element_type=jnp.float32,
        )
        outgoing.append(requests_out.astype(jnp.int32))
        layouts.append((item_row_codes, is_cold, flat_index, slot_capacity))
    wanted_all = jnp.concatenate(outgoing, axis=1)
    cold_rows = jnp.take(
        cold_item_table,
        lax.all_to_all(wanted_all, "table", split_axis=0, concat_axis=0, tiled=True),
        axis=0,
    ).astype(jnp.bfloat16)
    fetched = lax.all_to_all(cold_rows, "table", split_axis=0, concat_axis=0, tiled=True)
    results = []
    column_start = 0
    for item_row_codes, is_cold, flat_index, slot_capacity in layouts:
        flat_rows = fetched[:, column_start : column_start + slot_capacity].reshape(
            table_row_count * slot_capacity, fetched.shape[2]
        )
        picked = jnp.take(flat_rows, jnp.where(is_cold, flat_index, 0), axis=0)
        hot_rows = jnp.take(hot_item_table, jnp.where(is_cold, 0, item_row_codes), axis=0).astype(
            jnp.bfloat16
        )
        results.append(jnp.where(is_cold[:, None], picked, hot_rows))
        column_start = column_start + slot_capacity
    return results


def body(
    hot_item_table, cold_item_table, hist_rows, cand_rows, w_query, w_key, w_first, w_second, w_out
):
    table_row_count = lax.axis_size("table")
    requests, h_dev = hist_rows.shape
    c_dev = cand_rows.shape[1]
    width = hot_item_table.shape[1]
    cap_h = max(2, requests * h_dev // table_row_count)
    cap_c = max(2, requests * c_dev // table_row_count)
    history_emb, candidate_emb = gather_owner_rows(
        [hist_rows.reshape(-1), cand_rows.reshape(-1)],
        [cap_h, cap_c],
        hot_item_table,
        cold_item_table,
        table_row_count,
    )
    candidate_bf = candidate_emb.reshape(requests, c_dev, width)
    queries = jnp.einsum(
        "rce,ea->rca", candidate_bf, w_query, preferred_element_type=jnp.float32
    ).astype(jnp.bfloat16)
    score_scale = 1.0 / math.sqrt(w_query.shape[1])
    history_bf = history_emb.reshape(requests, h_dev, width)
    shard_rows = lax.all_gather(history_bf, "score", axis=1, tiled=True)
    key_rows = jnp.einsum(
        "rhe,ea->rha", shard_rows, w_key, preferred_element_type=jnp.float32
    ).astype(jnp.bfloat16)
    logits = (
        jnp.einsum("rca,rha->rch", queries, key_rows, preferred_element_type=jnp.float32)
        * score_scale
    )
    weights = jax.nn.sigmoid(logits).astype(jnp.bfloat16)
    pooled_sum = jnp.einsum("rch,rhe->rce", weights, shard_rows, preferred_element_type=jnp.float32)
    pooled = (pooled_sum * (1.0 / math.sqrt(H))).astype(jnp.bfloat16)
    joined = jnp.concatenate([candidate_bf, pooled], axis=2).reshape(requests * c_dev, 2 * width)
    hidden = jnp.maximum(jnp.dot(joined, w_first, preferred_element_type=jnp.float32), 0.0).astype(
        jnp.bfloat16
    )
    hidden = jnp.maximum(
        jnp.dot(hidden, w_second[0], preferred_element_type=jnp.float32), 0.0
    ).astype(jnp.bfloat16)
    ranked = jnp.dot(hidden, w_out, preferred_element_type=jnp.float32)
    return ranked.reshape(requests, c_dev)


def solution(mesh):
    return jax.shard_map(
        body,
        mesh=mesh,
        in_specs=(
            P(),
            P("table", None),
            P("table", "score"),
            P("table", "score"),
            P(),
            P(),
            P(),
            P(),
            P(),
        ),
        out_specs=P("table", "score"),
        check_vma=False,
    )
```

profile of v0, /device:TPU:0, one launch (start us, length us, event | category | flops | bytes accessed | tf_op | source)
XLA Modules:
  0.0 134.3 jit_solution(15087299233577586099)
XLA Ops:
  6.5 0.0 copy-start
  6.5 0.9 broadcast_compare_fusion.1
  7.4 0.7 broadcast_add_fusion.1
  8.1 0.7 broadcast_compare_fusion
  8.8 0.7 broadcast_add_fusion
  9.5 0.1 convert_reduce_fusion.1
  9.7 0.1 fusion.49
  9.8 0.2 fusion.7
  10.0 0.7 copy.13
  10.8 0.1 convert_reduce_fusion
  10.9 0.1 fusion.48
  11.0 0.2 fusion.6
  11.2 0.7 copy.12
  12.0 2.1 %convolution_convert_fusion.3 = s32[16,128]{1,0:T(8,128)S(1)} fusion(s32[2048]{0:T(1024)S(1)} %convert_bitcast_fusion.1, f32[2048]{0:T(1024)S(1)} %get-tuple-element.16, s32[2048]{0:T(1024)S(1)} %get-tuple-element.8, pred[2048]{0:T(1024)(128)(4,1)S(1)} %get-tuple-element.9), kind=kOutput, calls=%fused_computation.23 | convolution fusion | flops 50694144 | bytes 34816 | tf_op jit(solution)/shard_map/io,is->os/dot_general | solution.py:58
  14.1 2.1 %convolution_convert_fusion.2 = s32[16,128]{1,0:T(8,128)S(1)} fusion(s32[2048]{0:T(1024)S(1)} %convert_bitcast_fusion, f32[2048]{0:T(1024)S(1)} %get-tuple-element.17, s32[2048]{0:T(1024)S(1)} %get-tuple-element.11, pred[2048]{0:T(1024)(128)(4,1)S(1)} %get-tuple-element.12), kind=kOutput, calls=%fused_computation.22 | convolution fusion | flops 50694144 | bytes 34816 | tf_op jit(solution)/shard_map/io,is->os/dot_general | solution.py:58
  16.2 15.4 %all_to_all.20 = s32[16,1,256]{2,1,0:T(1,128)S(1)} all-to-all(s32[16,1,256]{2,1,0:T(1,128)S(1)} %copy.10), channel_id=1, replica_groups=mesh['table'=16,'score'=2] {'table'}, dimensions={0} | all-to-all | bytes 32768 | tf_op jit(solution)/shard_map/all_to_all | solution.py:70
  31.7 0.0 copy-done.1
  31.7 14.2 %gather_fusion = bf16[4096,128]{1,0:T(8,128)(2,1)} fusion(f32[1024,128]{1,0:T(8,128)S(1)} %copy-done.1, s32[4096]{0:T(1024)S(1)} %broadcast_clamp_fusion), kind=kCustom, calls=%fused_computation.4 | custom fusion | bytes 2113536 | tf_op jit(solution)/shard_map/jit(_take)/gather | solution.py:68
  46.0 2.6 %select_convert_fusion = bf16[16,256,128]{2,1,0:T(8,128)(2,1)} fusion(bf16[16,256,128]{2,1,0:T(8,128)(2,1)} %bitcast.70, pred[16,256]{1,0:T(8,128)(4,1)S(1)} %compare_and_fusion), kind=kLoop, calls=%fused_computation.9 | loop fusion | flops 524288 | bytes 2101248 | tf_op jit(solution)/shard_map/convert_element_type | solution.py:72
  48.6 4.3 %all-to-all-start.1 = ((bf16[16,256,128]{2,1,0:T(8,128)(2,1)}), bf16[16,256,128]{2,1,0:T(8,128)(2,1)}, u32[]{:S(2)}, u32[]{:S(2)}) async-start(bf16[16,256,128]{2,1,0:T(8,128)(2,1)} %select_convert_fusion), calls=%async_computation.1 | async-start | bytes 2097152 | tf_op jit(solution)/shard_map/all_to_all | solution.py:73
  53.0 0.2 all-gather.2.cloned.1.call-start
  53.2 0.0 copy-done.2
  53.2 7.6 %gather_fusion.4 = bf16[2048,128]{1,0:T(8,128)(2,1)} fusion(f32[2048,128]{1,0:T(8,128)S(1)} %copy-done.2, s32[2048]{0:T(1024)S(1)} %get-tuple-element.15), kind=kCustom, calls=%fused_computation.3.clone | custom fusion | bytes 1056768 | tf_op jit(solution)/shard_map/jit(_take)/gather | solution.py:81
  60.8 15.4 %all-to-all-done.1 = bf16[16,256,128]{2,1,0:T(8,128)(2,1)} async-done(((bf16[16,256,128]{2,1,0:T(8,128)(2,1)}), bf16[16,256,128]{2,1,0:T(8,128)(2,1)}, u32[]{:S(2)}, u32[]{:S(2)}) %all-to-all-start.1) | async-done | bytes 1048608 | tf_op jit(solution)/shard_map/all_to_all | solution.py:73
  76.3 2.3 %fusion.61 = (bf16[16,128,128]{2,1,0:T(8,128)(2,1)}, bf16[16,128,128]{2,1,0:T(8,128)(2,1)}) fusion(bf16[16,256,128]{2,1,0:T(8,128)(2,1)} %all-to-all-done.1), kind=kLoop, calls=%fused_computation.131 | loop fusion | bytes 2097152 | tf_op jit(solution)/shard_map/slice | solution.py:77
  78.6 8.8 %gather_fusion.3 = bf16[2048,128]{1,0:T(8,128)(2,1)} fusion(bf16[2048,128]{1,0:T(8,128)(2,1)} %bitcast.69, s32[2048]{0:T(1024)S(1)} %get-tuple-element.19), kind=kCustom, calls=%fused_computation.2.clone | custom fusion | bytes 1056768 | tf_op jit(solution)/shard_map/jit(_take)/gather | solution.py:80
  87.3 4.0 %fusion.21 = bf16[2048,128]{1,0:T(8,128)(2,1)} fusion(bf16[2048,128]{1,0:T(8,128)(2,1)} %gather_fusion.4, bf16[2048,128]{1,0:T(8,128)(2,1)} %gather_fusion.3, pred[2048]{0:T(1024)(128)(4,1)S(1)} %compare_and_fusion.1, pred[2048]{0:T(1024)(128)(4,1)S(1)} %get-tuple-element.6, pred[2048]{0:T(1024)(128)(4,1)S(1)} %get-tuple-element.9), kind=kLoop, calls=%fused_computation.38 | loop fusion | flops 786432 | bytes 1579008 | tf_op jit(solution)/shard_map/jit(_where)/select_n | solution.py:84
  91.4 0.0 all-gather.2.cloned.1.call-update
  91.4 7.6 %gather_fusion.2 = bf16[2048,128]{1,0:T(8,128)(2,1)} fusion(f32[2048,128]{1,0:T(8,128)S(1)} %copy-done.2, s32[2048]{0:T(1024)S(1)} %get-tuple-element.18), kind=kCustom, calls=%fused_computation.1.clone | custom fusion | bytes 1056768 | tf_op jit(solution)/shard_map/jit(_take)/gather | solution.py:81
  99.0 0.0 copy-done.7
  99.0 0.0 copy-start.8
  99.1 6.9 %gather_fusion.1 = bf16[2048,128]{1,0:T(8,128)(2,1)S(1)} fusion(bf16[2048,128]{1,0:T(8,128)(2,1)} %bitcast.68, s32[2048]{0:T(1024)S(1)} %get-tuple-element.20), kind=kCustom, calls=%fused_computation.clone | custom fusion | bytes 1056768 | tf_op jit(solution)/shard_map/jit(_take)/gather | solution.py:80
  106.0 0.0 copy-done.3
  106.0 1.6 %fusion.20 = bf16[2048,128]{1,0:T(8,128)(2,1)S(1)} fusion(bf16[2048,128]{1,0:T(8,128)(2,1)S(1)} %copy-done.3, bf16[2048,128]{1,0:T(8,128)(2,1)S(1)} %gather_fusion.1, pred[2048]{0:T(1024)(128)(4,1)S(1)} %compare_and_fusion.3, pred[2048]{0:T(1024)(128)(4,1)S(1)} %get-tuple-element.10, pred[2048]{0:T(1024)(128)(4,1)S(1)} %get-tuple-element.12), kind=kLoop, calls=%fused_computation.37 | loop fusion | flops 786432 | bytes 1579008 | tf_op jit(solution)/shard_map/jit(_where)/select_n | solution.py:84
  107.6 0.0 copy-start.4
  107.6 0.8 copy-done.4
  108.4 0.0 copy-done.6
  108.4 0.3 convolution_convert_fusion.1
  108.7 0.0 copy-start.5
  108.7 0.0 all-gather.2.cloned.1.call-done
  108.7 0.0 copy-done.8
  108.7 4.0 %divide_convert_fusion = bf16[8,256,512]{2,1,0:T(8,128)(2,1)} fusion(bf16[8,256,128]{2,1,0:T(8,128)(2,1)S(1)} %convolution_convert_fusion.1, bf16[8,512,128]{2,1,0:T(8,128)(2,1)} %all-gather.2.cloned.1.call-done, bf16[128,128]{1,0:T(8,128)(2,1)S(1)} %copy-done.8), kind=kOutput, calls=%fused_computation.7 | convolution fusion | flops 408420352 | bytes 3702784 | tf_op jit(solution)/shard_map/rca,rha->rch/dot_general | solution.py:116
  112.8 2.5 %fusion.1 = bf16[8,256,128]{2,1,0:T(8,128)(2,1)S(1)} fusion(bf16[8,256,512]{2,1,0:T(8,128)(2,1)} %divide_convert_fusion, bf16[8,512,128]{2,1,0:T(8,128)(2,1)} %all-gather.2.cloned.1.call-done), kind=kOutput, calls=%fused_computation.13 | convolution fusion | flops 268959744 | bytes 3670016 | tf_op jit(solution)/shard_map/rch,rhe->rce/dot_general | solution.py:120
  115.4 0.0 copy-done
  115.4 0.0 copy-done.5
  115.4 8.1 %maximum_convert_fusion = bf16[2048,1024]{1,0:T(8,128)(2,1)} fusion(bf16[1,1024,1024]{2,1,0:T(8,128)(2,1)S(1)} %copy-done, bf16[256,1024]{1,0:T(8,128)(2,1)} %param.19, bf16[2048,128]{1,0:T(8,128)(2,1)S(1)} %bitcast.83, bf16[2048,128]{1,0:T(8,128)(2,1)S(1)} %copy-done.5), kind=kOutput, calls=%fused_computation.5 | convolution fusion | flops 5379194880 | bytes 7864320 | tf_op jit(solution)/shard_map/dot_general | solution.py:127
  123.5 3.4 %fusion.62 = f32[1,2048]{1,0:T(1,128)S(1)} fusion(bf16[2048,1024]{1,0:T(8,128)(2,1)} %maximum_convert_fusion, bf16[1024,1]{0,1:T(2,128)(2,1)S(1)} %reshape.312), kind=kOutput, calls=%fused_computation.132 | convolution fusion | flops 4194304 | bytes 4204544 | tf_op jit(solution)/shard_map/dot_general | solution.py:129
  126.9 0.6 reshape.255
  (25 shorter events, 0.3 us)
Async XLA Ops:
  6.5 108.8 %copy-start = (bf16[1,1024,1024]{2,1,0:T(8,128)(2,1)S(1)}, bf16[1,1024,1024]{2,1,0:T(8,128)(2,1)}, u32[]{:S(2)}) copy-start(bf16[1,1024,1024]{2,1,0:T(8,128)(2,1)} %param.20) | copy-start | bytes 6291460
  6.5 25.2 %copy-start.1 = (f32[1024,128]{1,0:T(8,128)S(1)}, f32[1024,128]{1,0:T(8,128)}, u32[]{:S(2)}) copy-start(f32[1024,128]{1,0:T(8,128)} %param.14) | copy-start | bytes 1572868
  46.0 7.2 %copy-start.2 = (f32[2048,128]{1,0:T(8,128)S(1)}, f32[2048,128]{1,0:T(8,128)}, u32[]{:S(2)}) copy-start(f32[2048,128]{1,0:T(8,128)} %param.13) | copy-start | bytes 3145732
  48.6 27.6 %all-to-all-start.1 = ((bf16[16,256,128]{2,1,0:T(8,128)(2,1)}), bf16[16,256,128]{2,1,0:T(8,128)(2,1)}, u32[]{:S(2)}, u32[]{:S(2)}) async-start(bf16[16,256,128]{2,1,0:T(8,128)(2,1)} %select_convert_fusion), calls=%async_computation.1 | async-start | bytes 2097152 | tf_op jit(solution)/shard_map/all_to_all | solution.py:73
  53.0 55.8 %all-gather.2.cloned.1.call-start = ((), (), s32[]{:S(2)}) async-start(), calls=%async_computation.2 | async-start | bytes 1572864 | tf_op jit(solution)/shard_map/all_gather | solution.py:111
  87.3 11.7 %copy-start.7 = (bf16[1024]{0:T(1024)(128)(2,1)S(1)}, bf16[1024]{0:T(1024)(128)(2,1)}, u32[]{:S(2)}) copy-start(bf16[1024]{0:T(1024)(128)(2,1)} %param.21) | copy-start | bytes 6148
  99.0 6.9 %copy-start.3 = (bf16[2048,128]{1,0:T(8,128)(2,1)S(1)}, bf16[2048,128]{1,0:T(8,128)(2,1)}, u32[]{:S(2)}) copy-start(bf16[2048,128]{1,0:T(8,128)(2,1)} %gather_fusion.2) | copy-start | bytes 1572868
  99.0 9.4 %copy-start.6 = (bf16[128,128]{1,0:T(8,128)(2,1)S(1)}, bf16[128,128]{1,0:T(8,128)(2,1)}, u32[]{:S(2)}) copy-start(bf16[128,128]{1,0:T(8,128)(2,1)} %param.17) | copy-start | bytes 98308
  99.0 9.7 %copy-start.8 = (bf16[128,128]{1,0:T(8,128)(2,1)S(1)}, bf16[128,128]{1,0:T(8,128)(2,1)}, u32[]{:S(2)}) copy-start(bf16[128,128]{1,0:T(8,128)(2,1)} %param.18) | copy-start | bytes 98308
  107.6 0.8 copy-start.4
  108.7 6.7 %copy-start.5 = (bf16[2048,128]{1,0:T(8,128)(2,1)S(1)}, bf16[2048,128]{1,0:T(8,128)(2,1)}, u32[]{:S(2)}) copy-start(bf16[2048,128]{1,0:T(8,128)(2,1)} %copy-done.4) | copy-start | bytes 1572868
Sparse Core Ops, SparseCore 0:
  91.5 9.2 all-gather.1
where the time goes:
time: 135 us; the launch traced here: 134 us
  local copies, waits for them, and re-layouts  50.4 us (37%)
  matrix products  23.2 us (17%)
  waiting for transfers between devices  15.5 us (11%)
  blocking collectives  15.4 us (11%)
  between operations  13.7 us (10%)
  other arithmetic  11.7 us (9%)
  starting transfers between devices  4.56 us (3%)
    gather x2, local copies, waits for them, and re-layouts, gather_owner_rows(): picked = jnp.take(flat_rows, jnp.where(is_cold, flat_index, 0), axis=0)  15.6 us
    all_to_all x1, blocking collectives, gather_owner_rows(): lax.all_to_all(wanted_all, 'table', split_axis=0, concat_axis=0, tiled=True)  15.4 us
    all_to_all x1, waiting for transfers between devices, gather_owner_rows(): lax.all_to_all(cold_rows, 'table', split_axis=0, concat_axis=0, tiled=True)  15.4 us
    gather x2, local copies, waits for them, and re-layouts, gather_owner_rows(): jnp.take(hot_item_table, jnp.where(is_cold, 0, item_row_codes), axis=0)  15.2 us
    gather x1, local copies, waits for them, and re-layouts, gather_owner_rows(): jnp.take(cold_item_table, lax.all_to_all(wanted_all, 'table', split_axis=...  14.2 us
    dot_general x1, matrix products, body(): jnp.dot(hidden, w_second[0], preferred_element_type=jnp.float32)  8.14 us
    select_n x2, other arithmetic, gather_owner_rows(): results.append(jnp.where(is_cold[:, None], picked, hot_rows))  5.69 us
    all_to_all x1, starting transfers between devices, gather_owner_rows(): lax.all_to_all(cold_rows, 'table', split_axis=0, concat_axis=0, tiled=True)  4.34 us
  transfers between devices with their start and end apart: 2, of which 1 were waited for; matrix products, arithmetic and copies ran while one was open for 18% of the time, Pallas kernels for 0%

commit v1 on v0

--- a/solution.py
+++ b/solution.py
@@ -7,6 +7,29 @@
 H = 512
 HOT = 2048
 COLD_DEV = 1024
+
+
+def cut_along(value, dim, length):
+    lengths = value.shape
+    pieces = value.reshape(*lengths[:dim], length, lengths[dim] // length, *lengths[dim + 1 :])
+    return jnp.moveaxis(pieces, dim, 0)
+
+
+def in_order(blocks, dim):
+    dims = list(blocks.shape[1:])
+    dims[dim] *= blocks.shape[0]
+    return jnp.moveaxis(blocks, 0, dim).reshape(dims)
+
+
+def rotated_exchange(x, axis, split_dim, concat_dim):
+    devices, index = (lax.axis_size(axis), lax.axis_index(axis))
+    pieces = cut_along(x, split_dim, devices)
+    outs = [pieces[index]]
+    for step in range(1, devices):
+        sent = pieces[(index + step) % devices]
+        outs.append(lax.ppermute(sent, axis, [(i, (i + step) % devices) for i in range(devices)]))
+    pieces = jnp.stack(outs)[(index - jnp.arange(devices)) % devices]
+    return in_order(pieces, concat_dim)
 
 
 def owner_positions(owner_match):
@@ -66,9 +89,7 @@
         layouts.append((item_row_codes, is_cold, flat_index, slot_capacity))
     wanted_all = jnp.concatenate(outgoing, axis=1)
     cold_rows = jnp.take(
-        cold_item_table,
-        lax.all_to_all(wanted_all, "table", split_axis=0, concat_axis=0, tiled=True),
-        axis=0,
+        cold_item_table, rotated_exchange(wanted_all, "table", 0, 0), axis=0
     ).astype(jnp.bfloat16)
     fetched = lax.all_to_all(cold_rows, "table", split_axis=0, concat_axis=0, tiled=True)
     results = []

time: 135 us -> 151 us (1.12)
  starting transfers between devices: 4.56 us -> 32.8 us
  blocking collectives: 15.4 us -> 0 us
  waiting for transfers between devices: 15.5 us -> 17.7 us
    ppermute x0 -> x15, starting transfers between devices: none -> 28 us  [rotated_exchange(): lax.ppermute(sent, axis, [(i, (i + step) % devices) for i in range(device...]
    all_to_all x1 -> x0, blocking collectives: 15.4 us -> none  [gather_owner_rows(): lax.all_to_all(wanted_all, 'table', split_axis=0, concat_axis=0, tiled=True)]
    ppermute x0 -> x15, waiting for transfers between devices: none -> 4.86 us  [rotated_exchange(): lax.ppermute(sent, axis, [(i, (i + step) % devices) for i in range(device...]
    all_to_all x1, waiting for transfers between devices: 15.4 us -> 12.8 us  [gather_owner_rows(): lax.all_to_all(cold_rows, 'table', split_axis=0, concat_axis=0, tiled=True)]
    gather x1 -> x2, local copies, waits for them, and re-layouts: 14.2 us -> 14.9 us  [the longest x1 14.3 us: gather_owner_rows(): jnp.take(cold_item_table, rotated_exchange(wanted_all, 'table', 0, 0), ax...]
  transfers between devices with their start and end apart: 2 -> 17, of which waited for: 1 -> 5; matrix products, arithmetic and copies ran while one was open for 18% -> 16% of each run, Pallas kernels for 0% -> 0%
where the time goes in v1:
time: 151 us; the launch traced here: 150 us
  local copies, waits for them, and re-layouts  51.1 us (34%)
  starting transfers between devices  32.8 us (22%)
  matrix products  23.2 us (15%)
  waiting for transfers between devices  17.7 us (12%)
  between operations  13.7 us (9%)
  other arithmetic  11.7 us (8%)
    ppermute x15, starting transfers between devices, rotated_exchange(): lax.ppermute(sent, axis, [(i, (i + step) % devices) for i in range(device...  28 us
    gather x2, local copies, waits for them, and re-layouts, gather_owner_rows(): picked = jnp.take(flat_rows, jnp.where(is_cold, flat_index, 0), axis=0)  15.6 us
    gather x2, local copies, waits for them, and re-layouts, gather_owner_rows(): jnp.take(hot_item_table, jnp.where(is_cold, 0, item_row_codes), axis=0)  15.4 us
    gather x1, local copies, waits for them, and re-layouts, gather_owner_rows(): jnp.take(cold_item_table, rotated_exchange(wanted_all, 'table', 0, 0), ax...  14.3 us
    all_to_all x1, waiting for transfers between devices, gather_owner_rows(): lax.all_to_all(cold_rows, 'table', split_axis=0, concat_axis=0, tiled=True)  12.8 us
    dot_general x1, matrix products, body(): jnp.dot(hidden, w_second[0], preferred_element_type=jnp.float32)  8.13 us
    select_n x2, other arithmetic, gather_owner_rows(): results.append(jnp.where(is_cold[:, None], picked, hot_rows))  5.72 us
    ppermute x15, waiting for transfers between devices, rotated_exchange(): lax.ppermute(sent, axis, [(i, (i + step) % devices) for i in range(device...  4.86 us
  transfers between devices with their start and end apart: 17, of which 5 were waited for; matrix products, arithmetic and copies ran while one was open for 16% of the time, Pallas kernels for 0%

profile of v1, /device:TPU:0, one launch (start us, length us, event | category | flops | bytes accessed | tf_op | source)
XLA Modules:
  0.0 150.2 jit_solution(11914817156686161932)
XLA Ops:
  6.5 0.9 broadcast_compare_fusion.1
  7.4 0.7 broadcast_add_fusion.1
  8.1 0.7 broadcast_compare_fusion
  8.8 0.7 broadcast_add_fusion
  9.8 0.2 fusion.7
  10.0 0.7 copy.11
  10.9 0.1 fusion.49
  11.0 0.2 fusion.6
  11.2 0.7 copy.10
  12.0 2.1 %convolution_convert_fusion.3 = s32[16,128]{1,0:T(8,128)S(1)} fusion(s32[2048]{0:T(1024)S(1)} %convert_bitcast_fusion.1, f32[2048]{0:T(1024)S(1)} %get-tuple-element.32, s32[2048]{0:T(1024)S(1)} %get-tuple-element.8, pred[2048]{0:T(1024)(128)(4,1)S(1)} %get-tuple-element.9), kind=kOutput, calls=%fused_computation.24 | convolution fusion | flops 50694144 | bytes 34816 | tf_op jit(solution)/shard_map/io,is->os/dot_general | solution.py:81
  14.1 2.1 %convolution_convert_fusion.2 = s32[16,128]{1,0:T(8,128)S(1)} fusion(s32[2048]{0:T(1024)S(1)} %convert_bitcast_fusion, f32[2048]{0:T(1024)S(1)} %get-tuple-element.33, s32[2048]{0:T(1024)S(1)} %get-tuple-element.11, pred[2048]{0:T(1024)(128)(4,1)S(1)} %get-tuple-element.12), kind=kOutput, calls=%fused_computation.23 | convolution fusion | flops 50694144 | bytes 34816 | tf_op jit(solution)/shard_map/io,is->os/dot_general | solution.py:81
  16.2 5.0 %collective-permute-start.9 = (s32[1,256]{1,0:T(1,128)S(1)}, s32[1,256]{1,0:T(1,128)S(1)}, u32[]{:S(2)}, u32[]{:S(2)}) collective-permute-start(s32[1,256]{1,0:T(1,128)S(1)} %get-tuple-element.28), channel_id=1, source_target_pairs={{0,20},{2,22},{4,24},{6,26},{8,28},{10,30},{12,0},{14,2},{16,4},{1... | collective-permute-start | bytes 3080 | tf_op jit(solution)/shard_map/ppermute | solution.py:30
  21.3 1.3 collective-permute-start.10
  22.6 1.4 collective-permute-start.11
  24.0 2.7 %collective-permute-start.12 = (s32[1,256]{1,0:T(1,128)S(1)}, s32[1,256]{1,0:T(1,128)S(1)}, u32[]{:S(2)}, u32[]{:S(2)}) collective-permute-start(s32[1,256]{1,0:T(1,128)S(1)} %get-tuple-element.27), channel_id=1, source_target_pairs={{0,26},{2,28},{4,30},{6,0},{8,2},{10,4},{12,6},{14,8},{16,10},{18,... | collective-permute-start | bytes 3080 | tf_op jit(solution)/shard_map/ppermute | solution.py:30
  26.7 1.2 collective-permute-start.4
  27.9 1.2 collective-permute-start.5
  29.2 2.1 %collective-permute-start.6 = (s32[1,256]{1,0:T(1,128)S(1)}, s32[1,256]{1,0:T(1,128)S(1)}, u32[]{:S(2)}, u32[]{:S(2)}) collective-permute-start(s32[1,256]{1,0:T(1,128)S(1)} %get-tuple-element.24), channel_id=1, source_target_pairs={{0,14},{2,16},{4,18},{6,20},{8,22},{10,24},{12,26},{14,28},{16,30}... | collective-permute-start | bytes 3080 | tf_op jit(solution)/shard_map/ppermute | solution.py:30
  31.3 1.3 collective-permute-start.7
  32.5 2.2 %collective-permute-start.8 = (s32[1,256]{1,0:T(1,128)S(1)}, s32[1,256]{1,0:T(1,128)S(1)}, u32[]{:S(2)}, u32[]{:S(2)}) collective-permute-start(s32[1,256]{1,0:T(1,128)S(1)} %get-tuple-element.26), channel_id=1, source_target_pairs={{0,18},{2,20},{4,22},{6,24},{8,26},{10,28},{12,30},{14,0},{16,2},{... | collective-permute-start | bytes 3080 | tf_op jit(solution)/shard_map/ppermute | solution.py:30
  34.7 5.5 %collective-permute-start.13 = (s32[1,256]{1,0:T(1,128)S(1)}, s32[1,256]{1,0:T(1,128)S(1)}, u32[]{:S(2)}, u32[]{:S(2)}) collective-permute-start(s32[1,256]{1,0:T(1,128)S(1)} %get-tuple-element.21), channel_id=1, source_target_pairs={{0,28},{2,30},{4,0},{6,2},{8,4},{10,6},{12,8},{14,10},{16,12},{18,... | collective-permute-start | bytes 3080 | tf_op jit(solution)/shard_map/ppermute | solution.py:30
  40.2 0.6 collective-permute-start.14
  40.8 1.5 collective-permute-start
  42.3 1.6 %collective-permute-start.2 = (s32[1,256]{1,0:T(1,128)S(1)}, s32[1,256]{1,0:T(1,128)S(1)}, u32[]{:S(2)}, u32[]{:S(2)}) collective-permute-start(s32[1,256]{1,0:T(1,128)S(1)} %get-tuple-element.19), channel_id=1, source_target_pairs={{0,6},{2,8},{4,10},{6,12},{8,14},{10,16},{12,18},{14,20},{16,22},{... | collective-permute-start | bytes 3080 | tf_op jit(solution)/shard_map/ppermute | solution.py:30
  43.8 0.5 collective-permute-start.3
  44.4 3.6 %collective-permute-done = s32[1,256]{1,0:T(1,128)S(1)} collective-permute-done((s32[1,256]{1,0:T(1,128)S(1)}, s32[1,256]{1,0:T(1,128)S(1)}, u32[]{:S(2)}, u32[]{:S(2)}) %collective-permute-start) | collective-permute-done | bytes 1056 | tf_op jit(solution)/shard_map/ppermute | solution.py:30
  47.9 0.6 collective-permute-done.1
  48.6 0.6 collective-permute-done.3
  49.3 0.6 gather_fusion
  49.9 14.3 %gather_fusion.1 = bf16[4096,128]{1,0:T(8,128)(2,1)} fusion(f32[1024,128]{1,0:T(8,128)S(1)} %copy-done.1, s32[4096]{0:T(1024)S(1)} %broadcast_clamp_fusion), kind=kCustom, calls=%fused_computation.5 | custom fusion | bytes 2113536 | tf_op jit(solution)/shard_map/jit(_take)/gather | solution.py:91
  64.3 2.6 %select_convert_fusion = bf16[16,256,128]{2,1,0:T(8,128)(2,1)} fusion(bf16[16,256,128]{2,1,0:T(8,128)(2,1)} %bitcast.87, pred[16,256]{1,0:T(8,128)(4,1)S(1)} %compare_and_fusion), kind=kLoop, calls=%fused_computation.10 | loop fusion | flops 524288 | bytes 2101248 | tf_op jit(solution)/shard_map/convert_element_type | solution.py:93
  66.9 4.6 %all-to-all-start = ((bf16[16,256,128]{2,1,0:T(8,128)(2,1)}), bf16[16,256,128]{2,1,0:T(8,128)(2,1)}, u32[]{:S(2)}, u32[]{:S(2)}) async-start(bf16[16,256,128]{2,1,0:T(8,128)(2,1)} %select_convert_fusion), calls=%async_computation | async-start | bytes 2097152 | tf_op jit(solution)/shard_map/all_to_all | solution.py:94
  71.4 0.2 all-gather.2.cloned.1.call-start
  71.7 7.7 %gather_fusion.5 = bf16[2048,128]{1,0:T(8,128)(2,1)} fusion(f32[2048,128]{1,0:T(8,128)S(1)} %copy-done.2, s32[2048]{0:T(1024)S(1)} %get-tuple-element.31), kind=kCustom, calls=%fused_computation.3.clone | custom fusion | bytes 1056768 | tf_op jit(solution)/shard_map/jit(_take)/gather | solution.py:102
  79.4 12.8 %all-to-all-done = bf16[16,256,128]{2,1,0:T(8,128)(2,1)} async-done(((bf16[16,256,128]{2,1,0:T(8,128)(2,1)}), bf16[16,256,128]{2,1,0:T(8,128)(2,1)}, u32[]{:S(2)}, u32[]{:S(2)}) %all-to-all-start) | async-done | bytes 1048608 | tf_op jit(solution)/shard_map/all_to_all | solution.py:94
  92.2 2.3 %fusion.81 = (bf16[16,128,128]{2,1,0:T(8,128)(2,1)}, bf16[16,128,128]{2,1,0:T(8,128)(2,1)}) fusion(bf16[16,256,128]{2,1,0:T(8,128)(2,1)} %all-to-all-done), kind=kLoop, calls=%fused_computation.188 | loop fusion | bytes 2097152 | tf_op jit(solution)/shard_map/slice | solution.py:98
  94.5 8.8 %gather_fusion.4 = bf16[2048,128]{1,0:T(8,128)(2,1)} fusion(bf16[2048,128]{1,0:T(8,128)(2,1)} %bitcast.86, s32[2048]{0:T(1024)S(1)} %get-tuple-element.35), kind=kCustom, calls=%fused_computation.2.clone | custom fusion | bytes 1056768 | tf_op jit(solution)/shard_map/jit(_take)/gather | solution.py:101
  103.3 4.1 %fusion.21 = bf16[2048,128]{1,0:T(8,128)(2,1)} fusion(bf16[2048,128]{1,0:T(8,128)(2,1)} %gather_fusion.5, bf16[2048,128]{1,0:T(8,128)(2,1)} %gather_fusion.4, pred[2048]{0:T(1024)(128)(4,1)S(1)} %compare_and_fusion.1, pred[2048]{0:T(1024)(128)(4,1)S(1)} %get-tuple-element.6, pred[2048]{0:T(1024)(128)(4,1)S(1)} %get-tuple-element.9), kind=kLoop, calls=%fused_computation.39 | loop fusion | flops 786432 | bytes 1579008 | tf_op jit(solution)/shard_map/jit(_where)/select_n | solution.py:105
  107.4 7.7 %gather_fusion.3 = bf16[2048,128]{1,0:T(8,128)(2,1)} fusion(f32[2048,128]{1,0:T(8,128)S(1)} %copy-done.2, s32[2048]{0:T(1024)S(1)} %get-tuple-element.34), kind=kCustom, calls=%fused_computation.1.clone | custom fusion | bytes 1056768 | tf_op jit(solution)/shard_map/jit(_take)/gather | solution.py:102
  115.1 6.7 %gather_fusion.2 = bf16[2048,128]{1,0:T(8,128)(2,1)S(1)} fusion(bf16[2048,128]{1,0:T(8,128)(2,1)} %bitcast.85, s32[2048]{0:T(1024)S(1)} %get-tuple-element.36), kind=kCustom, calls=%fused_computation.clone | custom fusion | bytes 1056768 | tf_op jit(solution)/shard_map/jit(_take)/gather | solution.py:101
  121.9 1.6 %fusion.20 = bf16[2048,128]{1,0:T(8,128)(2,1)S(1)} fusion(bf16[2048,128]{1,0:T(8,128)(2,1)S(1)} %copy-done.3, bf16[2048,128]{1,0:T(8,128)(2,1)S(1)} %gather_fusion.2, pred[2048]{0:T(1024)(128)(4,1)S(1)} %compare_and_fusion.3, pred[2048]{0:T(1024)(128)(4,1)S(1)} %get-tuple-element.10, pred[2048]{0:T(1024)(128)(4,1)S(1)} %get-tuple-element.12), kind=kLoop, calls=%fused_computation.38 | loop fusion | flops 786432 | bytes 1579008 | tf_op jit(solution)/shard_map/jit(_where)/select_n | solution.py:105
  123.6 0.8 copy-done.4
  124.3 0.3 convolution_convert_fusion.1
  124.7 4.0 %divide_convert_fusion = bf16[8,256,512]{2,1,0:T(8,128)(2,1)} fusion(bf16[8,256,128]{2,1,0:T(8,128)(2,1)S(1)} %convolution_convert_fusion.1, bf16[8,512,128]{2,1,0:T(8,128)(2,1)} %all-gather.2.cloned.1.call-done, bf16[128,128]{1,0:T(8,128)(2,1)S(1)} %copy-done.8), kind=kOutput, calls=%fused_computation.8 | convolution fusion | flops 408420352 | bytes 3702784 | tf_op jit(solution)/shard_map/rca,rha->rch/dot_general | solution.py:137
  128.7 2.5 %fusion.1 = bf16[8,256,128]{2,1,0:T(8,128)(2,1)S(1)} fusion(bf16[8,256,512]{2,1,0:T(8,128)(2,1)} %divide_convert_fusion, bf16[8,512,128]{2,1,0:T(8,128)(2,1)} %all-gather.2.cloned.1.call-done), kind=kOutput, calls=%fused_computation.14 | convolution fusion | flops 268959744 | bytes 3670016 | tf_op jit(solution)/shard_map/rch,rhe->rce/dot_general | solution.py:141
  131.3 8.1 %maximum_convert_fusion = bf16[2048,1024]{1,0:T(8,128)(2,1)} fusion(bf16[1,1024,1024]{2,1,0:T(8,128)(2,1)S(1)} %copy-done, bf16[256,1024]{1,0:T(8,128)(2,1)} %param.19, bf16[2048,128]{1,0:T(8,128)(2,1)S(1)} %bitcast.116, bf16[2048,128]{1,0:T(8,128)(2,1)S(1)} %copy-done.5), kind=kOutput, calls=%fused_computation.6 | convolution fusion | flops 5379194880 | bytes 7864320 | tf_op jit(solution)/shard_map/dot_general | solution.py:148
  139.4 3.4 %fusion.82 = f32[1,2048]{1,0:T(1,128)S(1)} fusion(bf16[2048,1024]{1,0:T(8,128)(2,1)} %maximum_convert_fusion, bf16[1024,1]{0,1:T(2,128)(2,1)S(1)} %reshape.410), kind=kOutput, calls=%fused_computation.189 | convolution fusion | flops 4194304 | bytes 4204544 | tf_op jit(solution)/shard_map/dot_general | solution.py:150
  142.8 0.6 reshape.341
  (59 shorter events, 0.8 us)
Async XLA Ops:
  6.5 124.7 %copy-start = (bf16[1,1024,1024]{2,1,0:T(8,128)(2,1)S(1)}, bf16[1,1024,1024]{2,1,0:T(8,128)(2,1)}, u32[]{:S(2)}) copy-start(bf16[1,1024,1024]{2,1,0:T(8,128)(2,1)} %param.20) | copy-start | bytes 6291460
  6.5 43.4 %copy-start.1 = (f32[1024,128]{1,0:T(8,128)S(1)}, f32[1024,128]{1,0:T(8,128)}, u32[]{:S(2)}) copy-start(f32[1024,128]{1,0:T(8,128)} %param.14) | copy-start | bytes 1572868
  16.2 11.7 %collective-permute-start.9 = (s32[1,256]{1,0:T(1,128)S(1)}, s32[1,256]{1,0:T(1,128)S(1)}, u32[]{:S(2)}, u32[]{:S(2)}) collective-permute-start(s32[1,256]{1,0:T(1,128)S(1)} %get-tuple-element.28), channel_id=1, source_target_pairs={{0,20},{2,22},{4,24},{6,26},{8,28},{10,30},{12,0},{14,2},{16,4},{1... | collective-permute-start | bytes 3080 | tf_op jit(solution)/shard_map/ppermute | solution.py:30
  21.3 7.9 %collective-permute-start.10 = (s32[1,256]{1,0:T(1,128)S(1)}, s32[1,256]{1,0:T(1,128)S(1)}, u32[]{:S(2)}, u32[]{:S(2)}) collective-permute-start(s32[1,256]{1,0:T(1,128)S(1)} %get-tuple-element.29), channel_id=1, source_target_pairs={{0,22},{2,24},{4,26},{6,28},{8,30},{10,0},{12,2},{14,4},{16,6},{18... | collective-permute-start | bytes 3080 | tf_op jit(solution)/shard_map/ppermute | solution.py:30
  22.6 8.7 %collective-permute-start.11 = (s32[1,256]{1,0:T(1,128)S(1)}, s32[1,256]{1,0:T(1,128)S(1)}, u32[]{:S(2)}, u32[]{:S(2)}) collective-permute-start(s32[1,256]{1,0:T(1,128)S(1)} %get-tuple-element.30), channel_id=1, source_target_pairs={{0,24},{2,26},{4,28},{6,30},{8,0},{10,2},{12,4},{14,6},{16,8},{18,... | collective-permute-start | bytes 3080 | tf_op jit(solution)/shard_map/ppermute | solution.py:30
  24.0 8.6 %collective-permute-start.12 = (s32[1,256]{1,0:T(1,128)S(1)}, s32[1,256]{1,0:T(1,128)S(1)}, u32[]{:S(2)}, u32[]{:S(2)}) collective-permute-start(s32[1,256]{1,0:T(1,128)S(1)} %get-tuple-element.27), channel_id=1, source_target_pairs={{0,26},{2,28},{4,30},{6,0},{8,2},{10,4},{12,6},{14,8},{16,10},{18,... | collective-permute-start | bytes 3080 | tf_op jit(solution)/shard_map/ppermute | solution.py:30
  26.7 8.0 %collective-permute-start.4 = (s32[1,256]{1,0:T(1,128)S(1)}, s32[1,256]{1,0:T(1,128)S(1)}, u32[]{:S(2)}, u32[]{:S(2)}) collective-permute-start(s32[1,256]{1,0:T(1,128)S(1)} %get-tuple-element.22), channel_id=1, source_target_pairs={{0,10},{2,12},{4,14},{6,16},{8,18},{10,20},{12,22},{14,24},{16,26}... | collective-permute-start | bytes 3080 | tf_op jit(solution)/shard_map/ppermute | solution.py:30
  27.9 12.2 %collective-permute-start.5 = (s32[1,256]{1,0:T(1,128)S(1)}, s32[1,256]{1,0:T(1,128)S(1)}, u32[]{:S(2)}, u32[]{:S(2)}) collective-permute-start(s32[1,256]{1,0:T(1,128)S(1)} %get-tuple-element.23), channel_id=1, source_target_pairs={{0,12},{2,14},{4,16},{6,18},{8,20},{10,22},{12,24},{14,26},{16,28}... | collective-permute-start | bytes 3080 | tf_op jit(solution)/shard_map/ppermute | solution.py:30
  29.2 11.6 %collective-permute-start.6 = (s32[1,256]{1,0:T(1,128)S(1)}, s32[1,256]{1,0:T(1,128)S(1)}, u32[]{:S(2)}, u32[]{:S(2)}) collective-permute-start(s32[1,256]{1,0:T(1,128)S(1)} %get-tuple-element.24), channel_id=1, source_target_pairs={{0,14},{2,16},{4,18},{6,20},{8,22},{10,24},{12,26},{14,28},{16,30}... | collective-permute-start | bytes 3080 | tf_op jit(solution)/shard_map/ppermute | solution.py:30
  31.3 11.0 %collective-permute-start.7 = (s32[1,256]{1,0:T(1,128)S(1)}, s32[1,256]{1,0:T(1,128)S(1)}, u32[]{:S(2)}, u32[]{:S(2)}) collective-permute-start(s32[1,256]{1,0:T(1,128)S(1)} %get-tuple-element.25), channel_id=1, source_target_pairs={{0,16},{2,18},{4,20},{6,22},{8,24},{10,26},{12,28},{14,30},{16,0},... | collective-permute-start | bytes 3080 | tf_op jit(solution)/shard_map/ppermute | solution.py:30
  32.5 9.7 %collective-permute-start.8 = (s32[1,256]{1,0:T(1,128)S(1)}, s32[1,256]{1,0:T(1,128)S(1)}, u32[]{:S(2)}, u32[]{:S(2)}) collective-permute-start(s32[1,256]{1,0:T(1,128)S(1)} %get-tuple-element.26), channel_id=1, source_target_pairs={{0,18},{2,20},{4,22},{6,24},{8,26},{10,28},{12,30},{14,0},{16,2},{... | collective-permute-start | bytes 3080 | tf_op jit(solution)/shard_map/ppermute | solution.py:30
  34.7 9.1 %collective-permute-start.13 = (s32[1,256]{1,0:T(1,128)S(1)}, s32[1,256]{1,0:T(1,128)S(1)}, u32[]{:S(2)}, u32[]{:S(2)}) collective-permute-start(s32[1,256]{1,0:T(1,128)S(1)} %get-tuple-element.21), channel_id=1, source_target_pairs={{0,28},{2,30},{4,0},{6,2},{8,4},{10,6},{12,8},{14,10},{16,12},{18,... | collective-permute-start | bytes 3080 | tf_op jit(solution)/shard_map/ppermute | solution.py:30
  40.2 4.2 %collective-permute-start.14 = (s32[1,256]{1,0:T(1,128)S(1)}, s32[1,256]{1,0:T(1,128)S(1)}, u32[]{:S(2)}, u32[]{:S(2)}) collective-permute-start(s32[1,256]{1,0:T(1,128)S(1)} %get-tuple-element.15), channel_id=1, source_target_pairs={{0,30},{2,0},{4,2},{6,4},{8,6},{10,8},{12,10},{14,12},{16,14},{18,... | collective-permute-start | bytes 3080 | tf_op jit(solution)/shard_map/ppermute | solution.py:30
  40.8 7.2 %collective-permute-start = (s32[1,256]{1,0:T(1,128)S(1)}, s32[1,256]{1,0:T(1,128)S(1)}, u32[]{:S(2)}, u32[]{:S(2)}) collective-permute-start(s32[1,256]{1,0:T(1,128)S(1)} %get-tuple-element.17), channel_id=1, source_target_pairs={{0,2},{2,4},{4,6},{6,8},{8,10},{10,12},{12,14},{14,16},{16,18},{18... | collective-permute-start | bytes 3080 | tf_op jit(solution)/shard_map/ppermute | solution.py:30
  42.3 6.3 %collective-permute-start.1 = (s32[1,256]{1,0:T(1,128)S(1)}, s32[1,256]{1,0:T(1,128)S(1)}, u32[]{:S(2)}, u32[]{:S(2)}) collective-permute-start(s32[1,256]{1,0:T(1,128)S(1)} %get-tuple-element.18), channel_id=1, source_target_pairs={{0,4},{2,6},{4,8},{6,10},{8,12},{10,14},{12,16},{14,18},{16,20},{1... | collective-permute-start | bytes 3080 | tf_op jit(solution)/shard_map/ppermute | solution.py:30
  42.3 6.3 %collective-permute-start.2 = (s32[1,256]{1,0:T(1,128)S(1)}, s32[1,256]{1,0:T(1,128)S(1)}, u32[]{:S(2)}, u32[]{:S(2)}) collective-permute-start(s32[1,256]{1,0:T(1,128)S(1)} %get-tuple-element.19), channel_id=1, source_target_pairs={{0,6},{2,8},{4,10},{6,12},{8,14},{10,16},{12,18},{14,20},{16,22},{... | collective-permute-start | bytes 3080 | tf_op jit(solution)/shard_map/ppermute | solution.py:30
  43.8 5.4 %collective-permute-start.3 = (s32[1,256]{1,0:T(1,128)S(1)}, s32[1,256]{1,0:T(1,128)S(1)}, u32[]{:S(2)}, u32[]{:S(2)}) collective-permute-start(s32[1,256]{1,0:T(1,128)S(1)} %get-tuple-element.20), channel_id=1, source_target_pairs={{0,8},{2,10},{4,12},{6,14},{8,16},{10,18},{12,20},{14,22},{16,24},... | collective-permute-start | bytes 3080 | tf_op jit(solution)/shard_map/ppermute | solution.py:30
  64.3 7.4 %copy-start.2 = (f32[2048,128]{1,0:T(8,128)S(1)}, f32[2048,128]{1,0:T(8,128)}, u32[]{:S(2)}) copy-start(f32[2048,128]{1,0:T(8,128)} %param.13) | copy-start | bytes 3145732
  66.9 25.3 %all-to-all-start = ((bf16[16,256,128]{2,1,0:T(8,128)(2,1)}), bf16[16,256,128]{2,1,0:T(8,128)(2,1)}, u32[]{:S(2)}, u32[]{:S(2)}) async-start(bf16[16,256,128]{2,1,0:T(8,128)(2,1)} %select_convert_fusion), calls=%async_computation | async-start | bytes 2097152 | tf_op jit(solution)/shard_map/all_to_all | solution.py:94
  71.4 53.2 %all-gather.2.cloned.1.call-start = ((), (), s32[]{:S(2)}) async-start(), calls=%async_computation.1 | async-start | bytes 1572864 | tf_op jit(solution)/shard_map/all_gather | solution.py:132
  103.3 11.8 %copy-start.7 = (bf16[1024]{0:T(1024)(128)(2,1)S(1)}, bf16[1024]{0:T(1024)(128)(2,1)}, u32[]{:S(2)}) copy-start(bf16[1024]{0:T(1024)(128)(2,1)} %param.21) | copy-start | bytes 6148
  115.1 6.8 %copy-start.3 = (bf16[2048,128]{1,0:T(8,128)(2,1)S(1)}, bf16[2048,128]{1,0:T(8,128)(2,1)}, u32[]{:S(2)}) copy-start(bf16[2048,128]{1,0:T(8,128)(2,1)} %gather_fusion.3) | copy-start | bytes 1572868
  115.1 9.2 %copy-start.6 = (bf16[128,128]{1,0:T(8,128)(2,1)S(1)}, bf16[128,128]{1,0:T(8,128)(2,1)}, u32[]{:S(2)}) copy-start(bf16[128,128]{1,0:T(8,128)(2,1)} %param.17) | copy-start | bytes 98308
  115.1 9.6 %copy-start.8 = (bf16[128,128]{1,0:T(8,128)(2,1)S(1)}, bf16[128,128]{1,0:T(8,128)(2,1)}, u32[]{:S(2)}) copy-start(bf16[128,128]{1,0:T(8,128)(2,1)} %param.18) | copy-start | bytes 98308
  123.6 0.8 copy-start.4
  124.6 6.6 %copy-start.5 = (bf16[2048,128]{1,0:T(8,128)(2,1)S(1)}, bf16[2048,128]{1,0:T(8,128)(2,1)}, u32[]{:S(2)}) copy-start(bf16[2048,128]{1,0:T(8,128)(2,1)} %copy-done.4) | copy-start | bytes 1572868
Sparse Core Ops, SparseCore 0:
  107.5 8.2 all-gather.1
